TPU v7x, 32 devices: a whole 2x2x4 slice. The times are simulated.
32 devices in a mesh: ctx: 8 (over y, x, core), head: 4 (over z).
Axes of the slice: x: 2, y: 2, z: 4, core: 2. Of those that a mesh axis runs over, the one named last changes fastest.
Arguments:
- queries: bfloat16 [16, 2048, 128], P('head', 'ctx'), may hold values from -110 to 110
- keys: bfloat16 [2, 2048, 128], P(None, 'ctx'), may hold values from -4 to 4
- values: bfloat16 [2, 2048, 128], P(None, 'ctx'), may hold values from -6 to 6
- d_out: bfloat16 [16, 2048, 128], P('head', 'ctx'), may hold values from -6 to 6
- doc_lengths: int32 [4], replicated, may hold values from 1 to 1024, 2048 in all
Outputs:
- d_queries: bfloat16 [16, 2048, 128], P('head', 'ctx')
- d_keys: bfloat16 [2, 2048, 128], P(None, ('ctx', 'head'))
- d_values: bfloat16 [2, 2048, 128], P(None, ('ctx', 'head'))
Inputs may be any that keep to these rules, and one draw needn't show every extreme that they name: `doc_lengths`: documents lie end to end in order and their lengths sum to 2048; one of them has exactly 1024 tokens.
All inputs are finite; a program needn't handle non-finite values.
Results may differ from a plain program's by a relative error of at most 0.025.
Values may be sent and summed in bfloat16 or wider, within the bound.
No kernel may reach another device: no remote copies, remote signals or barrier semaphores. Data moves between devices by JAX's collectives and lax.ppermute only.
A program may use at most 64 MiB of HBM per device.

v0:
```python
import functools
import math

import jax
import jax.numpy as jnp
from jax import lax
from jax.experimental import pallas as pl
from jax.experimental.pallas import tpu as pltpu
from jax.sharding import PartitionSpec as P

GROUP = 8
REACH = 4
MASKED = -1e30
NN = (((1,), (0,)), ((), ()))
VMEM = pl.BlockSpec(memory_space=pltpu.VMEM)
SMEM = pl.BlockSpec(memory_space=pltpu.SMEM)
bf16, f32, i32 = jnp.bfloat16, jnp.float32, jnp.int32


def dot(a, b, dims=NN):
    return lax.dot_general(a, b, dims, preferred_element_type=f32)


def shape(dims, dtype):
    return jax.ShapeDtypeStruct(dims, dtype)


def call(body, name, in_specs, outs, scratch=()):
    return pl.pallas_call(
        body,
        out_shape=outs,
        in_specs=in_specs,
        out_specs=(VMEM,) * len(outs),
        scratch_shapes=scratch,
        compiler_params=pltpu.CompilerParams(vmem_limit_bytes=20 * 2**20),
        cost_estimate=pl.CostEstimate(flops=2**20, bytes_accessed=2**10, transcendentals=0),
        name=name,
    )


def shifted(block, distance):
    count = lax.axis_size("ctx")
    route = [(i - distance, i) for i in range(count) if 0 <= i - distance < count]
    return lax.ppermute(block, "ctx", route)


def exchanged(block, axis, mask):
    count = math.prod(lax.axis_size(name) for name in axis) if isinstance(axis, tuple) else (
        lax.axis_size(axis))
    return lax.ppermute(block, axis, [(i, i ^ mask) for i in range(count)])


def both(rows_ref):
    heads = rows_ref.shape[0] // 2
    return rows_ref.at[:heads], rows_ref.at[heads:]


def second_core():
    return lax.rem(lax.axis_index("ctx"), 2) == 1


def doc_starts(lengths_ref, block, tokens):
    row_pos = block * tokens + lax.broadcasted_iota(i32, (1, tokens), 1)
    starts = jnp.zeros((1, tokens), i32)
    end = jnp.int32(0)
    for d in range(lengths_ref.shape[0]):
        end = end + lengths_ref[d]
        starts = jnp.where(row_pos >= end, end, starts)
    return starts


def unit(pair, key_block, starts, turned_ref, e_ref, dp_ref, stats_ref, causal=False):
    heads, (width, tokens) = turned_ref.shape[0] // 2, turned_ref.shape[1:]
    factor = width ** -0.5 * math.log2(math.e)
    key_iota = lax.broadcasted_iota(i32, (tokens, 1), 0)
    allowed = key_block * tokens + key_iota >= starts
    if causal:
        allowed = allowed & (key_iota <= lax.broadcasted_iota(i32, (1, tokens), 1))
    for h in range(heads):
        lanes = slice(h * tokens, (h + 1) * tokens)
        s = jnp.where(allowed, dot(pair[:, :width], turned_ref[h]), MASKED)
        top = jnp.max(s, axis=0, keepdims=True)
        e = jnp.exp2((s - top) * factor)
        dp = dot(pair[:, width:], turned_ref[heads + h])
        e_ref[:, lanes] = e
        dp_ref[:, lanes] = dp
        stats_ref[0:1, lanes] = top
        stats_ref[1:2, lanes] = jnp.sum(e, axis=0, keepdims=True)
        stats_ref[2:3, lanes] = jnp.sum(e * dp, axis=0, keepdims=True)


def turn(rows_ref, turned_ref):
    for at in range(rows_ref.shape[0]):
        turned_ref[at] = rows_ref[at].T


def rows_of(ref, first=0):
    return [ref[first + row:first + row + 1] for row in range(3)]


def joined(parts, factor):
    top = functools.reduce(jnp.maximum, [part[0] for part in parts])
    gains = [jnp.exp2((part[0] - top) * factor) for part in parts]
    total = sum(gain * part[1] for gain, part in zip(gains, parts))
    weighted = sum(gain * part[2] for gain, part in zip(gains, parts))
    return top, total, weighted


def own_unit_body(starts_ref, rows_ref, own_ref, turned_ref, e_ref, dp_ref, stats_ref):
    turn(rows_ref, turned_ref)
    unit(own_ref, lax.axis_index("ctx"), starts_ref[0:1], turned_ref, e_ref, dp_ref, stats_ref,
         causal=True)


def four_unit_body(starts_ref, turned_ref, four_ref, e_ref, dp_ref, stats_ref):
    here = lax.axis_index("ctx")
    unit(four_ref, here - 4, starts_ref[0:1], turned_ref, e_ref, dp_ref, stats_ref)


def side_unit_body(starts_ref, other_rows, own_ref, four_ref,
                   turned_ref, e_ref, dp_ref, stats_ref):
    turn(other_rows, turned_ref)
    side = jnp.where(second_core(), four_ref[...], own_ref[...])
    block = lax.axis_index("ctx") - jnp.where(second_core(), 4, 0)
    unit(side, block, starts_ref[1:2], turned_ref, e_ref, dp_ref, stats_ref)


def prepare_body(share, middle, lengths_in, keys_ref, values_ref, queries_ref, d_out_ref,
                 split_out, starts_ref, own_ref, rows_ref, lengths_ref, split_ref, sems):
    heads, tokens, width = queries_ref.shape
    group = lax.axis_index("head") // share
    lengths = pltpu.make_async_copy(lengths_in, lengths_ref, sems.at[0])
    copies = [
        pltpu.make_async_copy(keys_ref.at[group], own_ref.at[:, :width], sems.at[1]),
        pltpu.make_async_copy(values_ref.at[group], own_ref.at[:, width:], sems.at[2]),
        pltpu.make_async_copy(queries_ref, rows_ref.at[:heads], sems.at[3]),
        pltpu.make_async_copy(d_out_ref, rows_ref.at[heads:], sems.at[4]),
    ]
    for copy in [lengths] + copies:
        copy.start()
    lengths.wait()
    end, split = jnp.int32(0), jnp.int32(0)
    for d in range(lengths_ref.shape[0]):
        end = end + lengths_ref[d]
        split = jnp.where(end == middle, 1, split)
    split_ref[0] = split
    copies.append(pltpu.make_async_copy(split_ref, split_out, sems.at[5]))
    copies[-1].start()
    here = lax.axis_index("ctx")
    starts_ref[0:1] = doc_starts(lengths_ref, here, tokens)
    starts_ref[1:2] = doc_starts(lengths_ref, jnp.bitwise_xor(here, 1), tokens)
    for copy in copies:
        copy.wait()


def near_side_unit_body(starts_ref, other_rows, own_ref, turned_ref, e_ref, dp_ref, stats_ref):
    turn(other_rows, turned_ref)
    block = jnp.where(second_core(), -1, lax.axis_index("ctx"))
    unit(own_ref, block, starts_ref[1:2], turned_ref, e_ref, dp_ref, stats_ref)


def write_rows(ref, values):
    for row, value in enumerate(values):
        ref[row:row + 1] = value


def cross_unit_body(starts_ref, turned_ref, two_ref, stats_side,
                    e_ref, dp_ref, stats_ref, others_ref):
    factor = turned_ref.shape[1] ** -0.5 * math.log2(math.e)
    unit(two_ref, lax.axis_index("ctx") - 2, starts_ref[1:2], turned_ref,
         e_ref, dp_ref, stats_ref)
    write_rows(others_ref, joined([rows_of(stats_side), rows_of(stats_ref)], factor))
    others_ref[3:4] = jnp.zeros((1, others_ref.shape[1]), f32)


def two_unit_body(starts_ref, turned_ref, two_ref, *refs):
    earlier, (e_ref, dp_ref, stats_ref, mine_ref) = refs[:-4], refs[-4:]
    factor = turned_ref.shape[1] ** -0.5 * math.log2(math.e)
    unit(two_ref, lax.axis_index("ctx") - 2, starts_ref[0:1], turned_ref,
         e_ref, dp_ref, stats_ref)
    write_rows(mine_ref, joined([rows_of(ref) for ref in earlier + (stats_ref,)], factor))
    mine_ref[3:4] = jnp.zeros((1, mine_ref.shape[1]), f32)


def coefficients(here_ref, taken_ref, stats_refs, width):
    factor = width ** -0.5 * math.log2(math.e)
    top, total, weighted = joined([rows_of(here_ref), rows_of(taken_ref)], factor)
    inverse = 1.0 / total
    return [weighted * inverse] + [
        jnp.exp2((ref[0:1] - top) * factor) * inverse for ref in stats_refs]


def slopes(e_ref, dp_ref, gain, delta, p_ref, ds_ref):
    p = e_ref[...] * gain
    p_ref[...] = p.astype(bf16)
    ds_ref[...] = (p * (dp_ref[...] - delta)).astype(bf16)


def flat(ref):
    heads, tokens, width = ref.shape
    return ref[...].reshape(heads * tokens, width)


def add_terms(sum_ref, ds_ref, p_ref, rows_ref, fresh):
    q_ref, g_ref = both(rows_ref)
    width = q_ref.shape[-1]
    dk = dot(ds_ref[...], flat(q_ref)) * width ** -0.5
    dv = dot(p_ref[...], flat(g_ref))
    if fresh:
        sum_ref[:, :width] = dk
        sum_ref[:, width:] = dv
    else:
        sum_ref[:, :width] += dk
        sum_ref[:, width:] += dv


def my_terms_body(count, mine_ref, taken_ref, *refs):
    stats, refs = refs[:count], refs[count:]
    parts, rows_ref, refs = refs[:4], refs[4], refs[5:]
    coef_ref, ds_refs, sums, p_ref = refs[0], refs[1:3], refs[3:5], refs[5]
    coefs = coefficients(mine_ref, taken_ref, stats, rows_ref.shape[-1])
    write_rows(coef_ref, coefs)
    for at in range(2):
        slopes(parts[2 * at], parts[2 * at + 1], coefs[count - 1 + at], coefs[0], p_ref.at[at],
               ds_refs[at])
        add_terms(sums[at], ds_refs[at], p_ref.at[at], rows_ref, True)


def four_terms_body(others_ref, taken_ref, stats_side, stats_cross, e_side, dp_side,
                    other_rows, part_ref, coef_ref, terms_ref, sum_ref, p_ref, ds_ref):
    coefs = coefficients(others_ref, taken_ref, (stats_side, stats_cross), other_rows.shape[-1])
    write_rows(coef_ref, coefs)
    sum_ref[...] = part_ref[...]

    @pl.when(second_core())
    def _():
        slopes(e_side, dp_side, coef_ref[1:2], coef_ref[0:1], p_ref, ds_ref)
        add_terms(sum_ref, ds_ref, p_ref, other_rows, False)

    terms_ref[...] = sum_ref[...].astype(bf16)


def two_terms_body(coef_ref, e_cross, dp_cross, other_rows, part_ref,
                   terms_ref, ds_cross, p_ref, sum_ref):
    slopes(e_cross, dp_cross, coef_ref[2:3], coef_ref[0:1], p_ref, ds_cross)
    sum_ref[...] = part_ref[...]
    add_terms(sum_ref, ds_cross, p_ref, other_rows, False)
    terms_ref[...] = sum_ref[...].astype(bf16)


def slice_rows(ref, other):
    count = lax.axis_size("head")
    each = ref.shape[0] // count
    parity = jnp.bitwise_xor(lax.rem(lax.axis_index("head"), 2), other)
    return [ref[pl.ds(pl.multiple_of((2 * at + parity) * each, each), each)]
            for at in range(count // 2)]


def halve(sum_ref, kept_ref, given_ref):
    each = sum_ref.shape[0] // lax.axis_size("head")
    for other, out_ref in enumerate((kept_ref, given_ref)):
        for at, value in enumerate(slice_rows(sum_ref, other)):
            out_ref[at * each:(at + 1) * each] = value.astype(out_ref.dtype)


def halved_two_terms_body(others_ref, taken_ref, stats_side, stats_cross, e_cross, dp_cross,
                        other_rows, part_ref,
                        coef_ref, kept_ref, other_ref, ds_cross, p_ref, sum_ref):
    coefs = coefficients(others_ref, taken_ref, (stats_side, stats_cross), other_rows.shape[-1])
    write_rows(coef_ref, coefs)
    slopes(e_cross, dp_cross, coefs[2], coefs[0], p_ref, ds_cross)
    sum_ref[...] = part_ref[...]
    add_terms(sum_ref, ds_cross, p_ref, other_rows, False)
    halve(sum_ref, kept_ref, other_ref)


def near_own_terms_body(coef_ref, e_side, dp_side, other_rows, part_ref,
                        kept_ref, other_ref, ds_side, p_ref, sum_ref):
    slopes(e_side, dp_side, coef_ref[1:2], coef_ref[0:1], p_ref, ds_side)
    sum_ref[...] = part_ref[...]

    @pl.when(jnp.logical_not(second_core()))
    def _():
        add_terms(sum_ref, ds_side, p_ref, other_rows, False)

    halve(sum_ref, kept_ref, other_ref)


def far_four_terms_body(coef_ref, e_side, dp_side, other_rows, part_ref,
                        kept_ref, other_ref, sum_ref, p_ref, ds_ref):
    sum_ref[...] = part_ref[...]

    @pl.when(second_core())
    def _():
        slopes(e_side, dp_side, coef_ref[1:2], coef_ref[0:1], p_ref, ds_ref)
        add_terms(sum_ref, ds_ref, p_ref, other_rows, False)

    halve(sum_ref, kept_ref, other_ref)


def far_own_terms_body(mine_coef, coef_ref, e_own, dp_own, e_side, dp_side, rows_ref,
                       other_rows,
                       kept_ref, other_ref, ds_own, ds_side, p_ref, p_side, sum_ref):
    slopes(e_own, dp_own, mine_coef[1:2], mine_coef[0:1], p_ref, ds_own)
    add_terms(sum_ref, ds_own, p_ref, rows_ref, True)
    slopes(e_side, dp_side, coef_ref[1:2], coef_ref[0:1], p_side, ds_side)

    @pl.when(jnp.logical_not(second_core()))
    def _():
        add_terms(sum_ref, ds_side, p_side, other_rows, False)

    halve(sum_ref, kept_ref, other_ref)


def grads_body(own_ref, two_ref, ds_own, ds_two, ds_side, ds_cross, *refs):
    four_refs, (dq_ref, other_dq_ref) = refs[:-2], refs[-2:]
    width = dq_ref.shape[-1]
    keys, slope_refs = [own_ref[:, :width], two_ref[:, :width]], [ds_own, ds_two]
    side = keys[0]
    if four_refs:
        keys.append(four_refs[0][:, :width])
        slope_refs.append(four_refs[1])
        side = jnp.where(second_core(), keys[2], side)
    query_grads([side, keys[1]], [ds_side, ds_cross], other_dq_ref)
    query_grads(keys, slope_refs, dq_ref)


def add_others_body(use, sum_ref, pair_ref, four_ref, out_ref):
    taken = jnp.where(use(lax.axis_index("ctx")), four_ref[...].astype(f32), 0.0)
    out_ref[...] = sum_ref[...] + pair_ref[...].astype(f32) + taken


def relay_body(kept_ref, four_ref, two_ref, two_pair_ref, out_ref, sent_ref):
    ctx = lax.axis_index("ctx")
    taken = two_ref[...].astype(f32) + two_pair_ref[...].astype(f32)
    out_ref[...] = kept_ref[...] + jnp.where(ctx & 2 == 0, taken, 0.0)
    sent_ref[...] = (four_ref[...] + jnp.where(ctx & 6 == 6, taken, 0.0)).astype(bf16)


def near_first_sum_body(kept_ref, two_ref, two_pair_ref, out_ref):
    taken = two_ref[...].astype(f32) + two_pair_ref[...].astype(f32)
    out_ref[...] = kept_ref[...] + jnp.where(lax.axis_index("ctx") & 2 == 0, taken, 0.0)


def halves_sum_body(share, use, kept_ref, back_ref, here_ref, there_ref):
    each = here_ref.shape[0]
    group = lax.axis_index("head") // share
    for out_ref, at in ((here_ref, group), (there_ref, 1 - group)):
        rows = pl.ds(pl.multiple_of(at * each, each), each)
        taken = back_ref[rows].astype(f32)
        if use is not None:
            taken = jnp.where(use(lax.axis_index("ctx")), taken, 0.0)
        out_ref[...] = (kept_ref[rows] + taken).astype(out_ref.dtype)


def last_body(share, here_ref, taken_ref, dk_ref, dv_ref):
    width = dk_ref.shape[-1]
    group = lax.axis_index("head") // share
    for ref, place in ((here_ref, group), (taken_ref, 1 - group)):
        dk_ref[place] = ref[:, :width]
        dv_ref[place] = ref[:, width:]


def query_grads(keys, ds_refs, out_ref):
    heads, tokens, width = out_ref.shape
    turned = [key.T for key in keys]
    for h in range(heads):
        lanes = slice(h * tokens, (h + 1) * tokens)
        dqt = sum(dot(kt, ds[:, lanes]) for kt, ds in zip(turned, ds_refs))
        out_ref[h] = (dqt.T * width ** -0.5).astype(out_ref.dtype)


def own_terms_body(mine_coef, coef_ref, e_own, dp_own, e_side, dp_side, rows_ref,
                   other_rows, own_ref, two_ref, ds_two, ds_cross, four_ref, ds_four,
                   terms_ref, dq_ref, other_dq_ref, ds_own, ds_side, p_ref, p_side):
    width = dq_ref.shape[-1]
    own, two, four = [ref[:, :width] for ref in (own_ref, two_ref, four_ref)]
    slopes(e_side, dp_side, coef_ref[1:2], coef_ref[0:1], p_side, ds_side)
    query_grads([jnp.where(second_core(), four, own), two], [ds_side, ds_cross], other_dq_ref)
    slopes(e_own, dp_own, mine_coef[1:2], mine_coef[0:1], p_ref, ds_own)
    add_terms(terms_ref, ds_own, p_ref, rows_ref, True)

    @pl.when(jnp.logical_not(second_core()))
    def _():
        add_terms(terms_ref, ds_side, p_side, other_rows, False)

    query_grads([own, two, four], [ds_own, ds_two, ds_four], dq_ref)


def add_grads_body(mine_ref, taken_ref, dq_ref):
    dq_ref[...] = (mine_ref[...] + taken_ref[...].astype(f32)).astype(dq_ref.dtype)


def sums_body(own_terms, four_back, two_back, out_ref):
    taken = four_back[...].astype(f32) + two_back[...].astype(f32)
    out_ref[...] = (own_terms[...] + taken).astype(bf16)


def per_device(queries, keys, values, d_out, doc_lengths):
    ctx_count, (heads, tokens, width) = lax.axis_size("ctx"), queries.shape
    middle = ctx_count // 2 * tokens
    split, starts, own, rows = pl.pallas_call(
        functools.partial(prepare_body, GROUP // heads, middle),
        out_shape=(shape((1,), i32), shape((2, tokens), i32), shape((tokens, 2 * width), bf16),
                   shape((2 * heads, tokens, width), bf16)),
        in_specs=[pl.BlockSpec(memory_space=pl.ANY)] * 5,
        out_specs=(pl.BlockSpec(memory_space=pl.ANY), VMEM, VMEM, VMEM),
        scratch_shapes=[pltpu.SMEM(doc_lengths.shape, i32), pltpu.SMEM((1,), i32),
                        pltpu.SemaphoreType.DMA((6,))],
        name="prepare",
    )(*[pltpu.with_memory_space_constraint(value, pltpu.HBM)
        for value in (doc_lengths, keys, values, queries, d_out)])
    operands = (rows, own, starts)
    if ctx_count != 2 * REACH or lax.axis_size("head") * heads != 2 * GROUP or 2 * heads != GROUP:
        return gradients(True, *operands)
    return lax.switch(split[0], [functools.partial(gradients, True),
                                 functools.partial(gradients, False)], *operands)


def gradients(far, row_data, own, starts):
    heads, (tokens, width) = row_data.shape[0] // 2, row_data.shape[1:]
    head_count = lax.axis_size("head")
    share = GROUP // heads
    groups = head_count // share
    rows = heads * tokens
    ctx = lax.axis_index("ctx")
    mutual = lax.axis_size("ctx") == 2 * REACH and share == groups == 2
    pair = (tokens, 2 * width)
    all_rows = (heads, tokens, width)
    stats = shape((3, rows), f32)
    wide = shape((tokens, rows), f32)
    half = shape((tokens, rows), bf16)
    half_scratch = pltpu.VMEM((tokens, rows), bf16)
    halves_scratch = pltpu.VMEM((2, tokens, rows), bf16)
    pair_scratch = pltpu.VMEM(pair, f32)

    if far:
        four = exchanged(own, "ctx", 4) if mutual else shifted(own, 4)
    two = [exchanged(own, "ctx", 6)] if far and mutual else []
    two.append(exchanged(own, "ctx", 2) if mutual else shifted(own, 2))
    flipped = shape((2 * heads, width, tokens), bf16)
    turned, e_own, dp_own, stats_own = call(
        own_unit_body, "own_unit", [VMEM] * 3, (flipped, wide, wide, stats),
    )(starts, row_data, own)
    other_rows = exchanged(row_data, "ctx", 1)
    if far:
        four, stats_own = lax.optimization_barrier((four, stats_own))
        e_four, dp_four, stats_four = call(
            four_unit_body, "four_unit", [VMEM] * 3, (wide, wide, stats))(starts, turned, four)
        other_rows, stats_four = lax.optimization_barrier((other_rows, stats_four))
        other_turned, e_side, dp_side, stats_side = call(
            side_unit_body, "side_unit", [VMEM] * 4, (flipped, wide, wide, stats),
        )(starts, other_rows, own, four)
    else:
        other_turned, e_side, dp_side, stats_side = call(
            near_side_unit_body, "side_unit", [VMEM] * 3, (flipped, wide, wide, stats),
        )(starts, other_rows, own)
    *two, stats_side, stats_own = lax.optimization_barrier((*two, stats_side, stats_own))
    mine_stats = (stats_own, stats_four) if far else (stats_own,)
    two = jnp.where(ctx & 2 == 2, two[1], two[0]) if len(two) == 2 else two[0]
    few = shape((4, rows), f32)
    e_cross, dp_cross, stats_cross, others = call(
        cross_unit_body, "cross_unit", [VMEM] * 4, (wide, wide, stats, few),
    )(starts, other_turned, two, stats_side)
    taken_others = exchanged(others, "ctx", 1)
    e_two, dp_two, stats_two, mine = call(
        two_unit_body, "two_unit", [VMEM] * (3 + len(mine_stats)), (wide, wide, stats, few),
    )(starts, turned, two, *mine_stats)
    taken_mine = exchanged(mine, "ctx", 1)
    mine_stats += (stats_two,)
    parts = ((e_four, dp_four) if far else (e_own, dp_own)) + (e_two, dp_two)
    mine_coef, ds_first, ds_two, first_part, two_part = call(
        functools.partial(my_terms_body, len(mine_stats)), "my_terms",
        [VMEM] * (7 + len(mine_stats)),
        (few, half, half, shape(pair, f32), shape(pair, f32)), (halves_scratch,),
    )(mine, taken_others, *mine_stats, *parts, row_data)
    last_stats = (others, taken_mine, stats_side, stats_cross)
    slices = (tokens // 2, 2 * width)
    slice_dims = (tokens // head_count, 2 * width)
    if not mutual:
        coef, four_terms = call(
            four_terms_body, "four_terms", [VMEM] * 8, (few, shape(pair, bf16)),
            (pair_scratch, half_scratch, half_scratch),
        )(*last_stats, e_side, dp_side, other_rows, first_part)
        two_terms, ds_cross = call(
            two_terms_body, "two_terms", [VMEM] * 5, (shape(pair, bf16), half),
            (half_scratch, pair_scratch),
        )(coef, e_cross, dp_cross, other_rows, two_part)
        backs = [shifted(four_terms, -4), shifted(two_terms, -2)]
        own_terms, my_grads, other_grads = call(
            own_terms_body, "own_terms", [VMEM] * 14,
            (shape(pair, f32), shape(all_rows, f32), shape(all_rows, bf16)),
            (half_scratch,) * 4,
        )(mine_coef, coef, e_own, dp_own, e_side, dp_side, row_data, other_rows, own, two,
          ds_two, ds_cross, four, ds_first)
        taken_grads = exchanged(other_grads, "ctx", 1)
        d_queries, = call(
            add_grads_body, "add_grads", [VMEM] * 2, (shape(all_rows, bf16),),
        )(my_grads, taken_grads)
        sums, = call(sums_body, "sums", [VMEM] * 3, (shape(pair, bf16),))(own_terms, *backs)
        pieces = lax.all_to_all(sums.reshape(head_count, *slice_dims), "head", 0, 0)
        result = jnp.sum(
            pieces.reshape(groups, share, *slice_dims).astype(f32), axis=1).astype(bf16)
        return d_queries, result[..., :width], result[..., width:]

    halves = (shape(slices, bf16), shape(slices, bf16))
    part = shape(slices, f32)
    coef, two_kept, two_other, ds_cross = call(
        halved_two_terms_body, "two_terms", [VMEM] * 8, (few,) + halves + (half,),
        (half_scratch, pair_scratch),
    )(*last_stats, e_cross, dp_cross, other_rows, two_part)
    two_back = exchanged(two_kept, "ctx", 2)
    two_pair = exchanged(two_other, ("ctx", "head"), 2 * head_count + 1)
    if far:
        four_kept, four_other = call(
            far_four_terms_body, "four_terms", [VMEM] * 5, (part, halves[1]),
            (pair_scratch, half_scratch, half_scratch),
        )(coef, e_side, dp_side, other_rows, first_part)
        four_pair = exchanged(four_other, ("ctx", "head"), 4 * head_count + 1)
        own_kept, own_other, ds_own, ds_side = call(
            far_own_terms_body, "own_terms", [VMEM] * 8, (part, halves[1], half, half),
            (half_scratch, half_scratch, pair_scratch),
        )(mine_coef, coef, e_own, dp_own, e_side, dp_side, row_data, other_rows)
    else:
        ds_own = ds_first
        own_kept, own_other, ds_side = call(
            near_own_terms_body, "own_terms", [VMEM] * 5, (part, halves[1], half),
            (half_scratch, pair_scratch),
        )(coef, e_side, dp_side, other_rows, first_part)
    own_pair = exchanged(own_other, "head", 1)
    four_refs = (four, ds_first) if far else ()
    my_grads, other_grads = call(
        grads_body, "query_grads", [VMEM] * (6 + len(four_refs)),
        (shape(all_rows, f32), shape(all_rows, bf16)),
    )(own, two, ds_own, ds_two, ds_side, ds_cross, *four_refs)
    owns_four = lambda i: i < 4
    if far:
        own_kept, relayed = call(
            relay_body, "relay", [VMEM] * 4, (part, halves[0]),
        )(own_kept, four_kept, two_back, two_pair)
        four_back = exchanged(relayed, "ctx", 4)
        own_kept, = call(functools.partial(add_others_body, owns_four), "add_others", [VMEM] * 3,
                         (part,))(own_kept, own_pair, four_pair)
        final, use = four_back, owns_four
    else:
        own_kept, = call(
            near_first_sum_body, "first_sum", [VMEM] * 3, (part,),
        )(own_kept, two_back, two_pair)
        final, use = own_pair, None
    kept, sent = call(
        functools.partial(halves_sum_body, share, use), "sums", [VMEM] * 2,
        (shape(slice_dims, bf16),) * 2)(own_kept, final)
    other_grads, kept = lax.optimization_barrier((other_grads, kept))
    taken_grads = exchanged(other_grads, "ctx", 1)
    d_queries, = call(
        add_grads_body, "add_grads", [VMEM] * 2, (shape(all_rows, bf16),),
    )(my_grads, taken_grads)
    last = exchanged(sent, "head", share)
    last, d_queries = lax.optimization_barrier((last, d_queries))
    d_keys, d_values = call(
        functools.partial(last_body, share), "last", [VMEM] * 2,
        (shape((groups, tokens // head_count, width), bf16),) * 2)(kept, last)
    return d_queries, d_keys, d_values


def solution(mesh):
    placed = (
        P("head", "ctx", None),
        P(None, "ctx", None),
        P(None, "ctx", None),
        P("head", "ctx", None),
        P(),
    )
    return jax.shard_map(
        per_device,
        mesh=mesh,
        in_specs=placed,
        out_specs=(
            P("head", "ctx", None),
            P(None, ("ctx", "head"), None),
            P(None, ("ctx", "head"), None),
        ),
        check_vma=False,
    )
```

profile of v0, /device:TPU:0, one launch (start us, length us, event | category | flops | bytes accessed | tf_op | source)
XLA Modules:
  0.0 34.6 jit_solution(18427600645794345544)
XLA Ops:
  0.6 1.2 %prepare.1 = (s32[1]{0:T(128)}, s32[2,256]{1,0:T(2,128)S(1)}, bf16[256,256]{1,0:T(8,128)(2,1)S(1)}, bf16[8,256,128]{2,1,0:T(8,128)(2,1)S(1)}) custom-call(s32[4]{0:T(128)} %lengths_in.1, bf16[2,256,128]{2,1,0:T(8,128)(2,1)} %keys_ref.1, bf16[2,256,128]{2,1,0:T(8,128)(2,1)} %values_ref.1, bf16[4,256,128]{2,1,0:T(8,128)(2,1)} %queries_ref.1, ...), custom_call_target="tpu_custom_call" | custom-call | tf_op jit(solution)/shard_map/prepare/pallas_call | solution.py:402
  2.5 32.0 %conditional.1 = (bf16[4,256,128]{2,1,0:T(8,128)(2,1)}, bf16[2,64,128]{2,1,0:T(8,128)(2,1)}, bf16[2,64,128]{2,1,0:T(8,128)(2,1)}) conditional(s32[]{:T(128)} %bitcast, (s32[2,256]{1,0:T(2,128)S(1)}, bf16[8,256,128]{2,1,0:T(8,128)(2,1)S(1)}, bf16[256,256]{1,0:T(8,128)(2,1)S(1)}) %tuple.23, (bf16[8,256,128]{2,1,0:T(8,128)(2,1)S(1)}, ...), branch_computations={%region_0.1_spmd, %region_1.2_spmd} | conditional | flops 15794181 | bytes 6700630 | solution.py:416
  2.5 0.5 %collective-permute-start.11 = (bf16[8,256,128]{2,1,0:T(8,128)(2,1)S(1)}, bf16[8,256,128]{2,1,0:T(8,128)(2,1)S(1)}, u32[]{:S(2)}, u32[]{:S(2)}) collective-permute-start(bf16[8,256,128]{2,1,0:T(8,128)(2,1)S(1)} %get-tuple-element.13.rows_ref.refs_7_), channel_id=1, source_target_pairs={{0,4},{4,0},{8,12},{12,8},{16,20},{20,16},{24,28},{28,24},{1,5},{5... | collective-permute-start | bytes 1572872 | tf_op jit(solution)/shard_map/cond/branch_0_fun/ppermute | solution.py:50
  3.1 2.6 %collective-permute-start.12 = (bf16[256,256]{1,0:T(8,128)(2,1)S(1)}, bf16[256,256]{1,0:T(8,128)(2,1)S(1)}, u32[]{:S(2)}, u32[]{:S(2)}) collective-permute-start(bf16[256,256]{1,0:T(8,128)(2,1)S(1)} %get-tuple-element.14.own_ref), channel_id=1, source_target_pairs={{0,16},{4,20},{8,24},{12,28},{16,0},{20,4},{24,8},{28,12},{1,17},{... | collective-permute-start | bytes 393224 | tf_op jit(solution)/shard_map/cond/branch_0_fun/ppermute | solution.py:50
  5.7 1.5 %collective-permute-start.10 = (bf16[256,256]{1,0:T(8,128)(2,1)S(1)}, bf16[256,256]{1,0:T(8,128)(2,1)S(1)}, u32[]{:S(2)}, u32[]{:S(2)}) collective-permute-start(bf16[256,256]{1,0:T(8,128)(2,1)S(1)} %get-tuple-element.14.own_ref), channel_id=1, source_target_pairs={{0,8},{4,12},{8,0},{12,4},{16,24},{20,28},{24,16},{28,20},{1,9},{5... | collective-permute-start | bytes 393224 | tf_op jit(solution)/shard_map/cond/branch_0_fun/ppermute | solution.py:50
  7.2 0.6 %own_unit.2 = (bf16[8,128,256]{2,1,0:T(8,128)(2,1)S(1)}, f32[256,1024]{1,0:T(8,128)S(1)}, f32[256,1024]{1,0:T(8,128)S(1)}, f32[3,1024]{1,0:T(4,128)S(1)}) custom-call(s32[2,256]{1,0:T(2,128)S(1)} %get-tuple-element.12.starts_ref, bf16[8,256,128]{2,1,0:T(8,128)(2,1)S(1)} %get-tuple-element.13.rows_ref.refs_7_, bf16[256,256]{1,0:T(8,128)(2,1)S(1)} %get-tuple-element.14.own_ref), custom_call_target="tpu_custom_call" | custom-call | flops 1048576 | bytes 1024 | tf_op jit(solution)/shard_map/cond/branch_0_fun/own_unit/pallas_call | solution.py:442
  7.8 1.9 %collective-permute-done.12.four_ref.refs_0_ = bf16[256,256]{1,0:T(8,128)(2,1)S(1)} collective-permute-done((bf16[256,256]{1,0:T(8,128)(2,1)S(1)}, bf16[256,256]{1,0:T(8,128)(2,1)S(1)}, u32[]{:S(2)}, u32[]{:S(2)}) %collective-permute-start.12) | collective-permute-done | bytes 131104 | tf_op jit(solution)/shard_map/cond/branch_0_fun/ppermute | solution.py:50
  9.7 0.6 %four_unit.1 = (f32[256,1024]{1,0:T(8,128)S(1)}, f32[256,1024]{1,0:T(8,128)S(1)}, f32[3,1024]{1,0:T(4,128)S(1)}) custom-call(s32[2,256]{1,0:T(2,128)S(1)} %get-tuple-element.12.starts_ref, bf16[8,128,256]{2,1,0:T(8,128)(2,1)S(1)} %get-tuple-element.15.turned_ref, bf16[256,256]{1,0:T(8,128)(2,1)S(1)} %collective-permute-done.12.four_ref.refs_0_), custom_call_target="tpu_custom_call" | custom-call | flops 1048576 | bytes 1024 | tf_op jit(solution)/shard_map/cond/branch_0_fun/four_unit/pallas_call | solution.py:448
  10.3 0.6 %side_unit.2 = (bf16[8,128,256]{2,1,0:T(8,128)(2,1)S(1)}, f32[256,1024]{1,0:T(8,128)S(1)}, f32[256,1024]{1,0:T(8,128)S(1)}, f32[3,1024]{1,0:T(4,128)S(1)}) custom-call(s32[2,256]{1,0:T(2,128)S(1)} %get-tuple-element.12.starts_ref, bf16[8,256,128]{2,1,0:T(8,128)(2,1)S(1)} %collective-permute-done.11.other_rows, ...), custom_call_target="tpu_custom_call" | custom-call | flops 1048576 | bytes 1024 | tf_op jit(solution)/shard_map/cond/branch_0_fun/side_unit/pallas_call | solution.py:451
  11.0 1.0 %collective-permute-done.10 = bf16[256,256]{1,0:T(8,128)(2,1)S(1)} collective-permute-done((bf16[256,256]{1,0:T(8,128)(2,1)S(1)}, bf16[256,256]{1,0:T(8,128)(2,1)S(1)}, u32[]{:S(2)}, u32[]{:S(2)}) %collective-permute-start.10) | collective-permute-done | bytes 131104 | tf_op jit(solution)/shard_map/cond/branch_0_fun/ppermute | solution.py:50
  12.0 1.7 %collective-permute-done.9 = bf16[256,256]{1,0:T(8,128)(2,1)S(1)} collective-permute-done((bf16[256,256]{1,0:T(8,128)(2,1)S(1)}, bf16[256,256]{1,0:T(8,128)(2,1)S(1)}, u32[]{:S(2)}, u32[]{:S(2)}) %collective-permute-start.9) | collective-permute-done | bytes 131104 | tf_op jit(solution)/shard_map/cond/branch_0_fun/ppermute | solution.py:50
  13.8 0.6 %cross_unit.2 = (f32[256,1024]{1,0:T(8,128)S(1)}, f32[256,1024]{1,0:T(8,128)S(1)}, f32[3,1024]{1,0:T(4,128)S(1)}, f32[4,1024]{1,0:T(4,128)S(1)}) custom-call(s32[2,256]{1,0:T(2,128)S(1)} %get-tuple-element.12.starts_ref, bf16[8,128,256]{2,1,0:T(8,128)(2,1)S(1)} %get-tuple-element.27.turned_ref, bf16[256,256]{1,0:T(8,128)(2,1)S(1)} %broadcast_select_fusion.two_ref, ...), custom_call_target="tpu_custom_call" | custom-call | flops 1048576 | bytes 1024 | tf_op jit(solution)/shard_map/cond/branch_0_fun/cross_unit/pallas_call | solution.py:462
  14.3 0.1 collective-permute-start.13
  14.4 0.6 %two_unit.2 = (f32[256,1024]{1,0:T(8,128)S(1)}, f32[256,1024]{1,0:T(8,128)S(1)}, f32[3,1024]{1,0:T(4,128)S(1)}, f32[4,1024]{1,0:T(4,128)S(1)}) custom-call(s32[2,256]{1,0:T(2,128)S(1)} %get-tuple-element.12.starts_ref, bf16[8,128,256]{2,1,0:T(8,128)(2,1)S(1)} %get-tuple-element.15.turned_ref, bf16[256,256]{1,0:T(8,128)(2,1)S(1)} %broadcast_select_fusion.two_ref, ...), custom_call_target="tpu_custom_call" | custom-call | flops 1048576 | bytes 1024 | tf_op jit(solution)/shard_map/cond/branch_0_fun/two_unit/pallas_call | solution.py:466
  15.0 0.6 %collective-permute-start.14 = (f32[4,1024]{1,0:T(4,128)S(1)}, f32[4,1024]{1,0:T(4,128)S(1)}, u32[]{:S(2)}, u32[]{:S(2)}) collective-permute-start(f32[4,1024]{1,0:T(4,128)S(1)} %get-tuple-element.26.mine_ref), channel_id=1, source_target_pairs={{0,4},{4,0},{8,12},{12,8},{16,20},{20,16},{24,28},{28,24},{1,5},{5... | collective-permute-start | bytes 49160 | tf_op jit(solution)/shard_map/cond/branch_0_fun/ppermute | solution.py:50
  15.6 0.8 %my_terms.2 = (f32[4,1024]{1,0:T(4,128)S(1)}, bf16[256,1024]{1,0:T(8,128)(2,1)S(1)}, bf16[256,1024]{1,0:T(8,128)(2,1)S(1)}, f32[256,256]{1,0:T(8,128)S(1)}, f32[256,256]{1,0:T(8,128)S(1)}) custom-call(f32[4,1024]{1,0:T(4,128)S(1)} %get-tuple-element.26.mine_ref, f32[4,1024]{1,0:T(4,128)S(1)} %collective-permute-done.13.taken_ref, ...), custom_call_target="tpu_custom_call" | custom-call | flops 1048576 | bytes 1024 | tf_op jit(solution)/shard_map/cond/branch_0_fun/my_terms/pallas_call | solution.py:472
  16.4 0.5 %two_terms.2 = (f32[4,1024]{1,0:T(4,128)S(1)}, bf16[128,256]{1,0:T(8,128)(2,1)S(1)}, bf16[128,256]{1,0:T(8,128)(2,1)S(1)}, bf16[256,1024]{1,0:T(8,128)(2,1)S(1)}) custom-call(f32[4,1024]{1,0:T(4,128)S(1)} %get-tuple-element.29.others_ref, f32[4,1024]{1,0:T(4,128)S(1)} %collective-permute-done.14.taken_ref, f32[3,1024]{1,0:T(4,128)S(1)} %get-tuple-element.28.stats_side, ...), custom_call_target="tpu_custom_call" | custom-call | flops 1048576 | bytes 1024 | tf_op jit(solution)/shard_map/cond/branch_0_fun/two_terms/pallas_call | solution.py:508
  16.9 1.8 %collective-permute-start.15 = (bf16[128,256]{1,0:T(8,128)(2,1)S(1)}, bf16[128,256]{1,0:T(8,128)(2,1)S(1)}, u32[]{:S(2)}, u32[]{:S(2)}) collective-permute-start(bf16[128,256]{1,0:T(8,128)(2,1)S(1)} %get-tuple-element.48), channel_id=1, source_target_pairs={{0,8},{4,12},{8,0},{12,4},{16,24},{20,28},{24,16},{28,20},{1,9},{5... | collective-permute-start | bytes 196616 | tf_op jit(solution)/shard_map/cond/branch_0_fun/ppermute | solution.py:50
  18.7 1.5 %collective-permute-start.16 = (bf16[128,256]{1,0:T(8,128)(2,1)S(1)}, bf16[128,256]{1,0:T(8,128)(2,1)S(1)}, u32[]{:S(2)}, u32[]{:S(2)}) collective-permute-start(bf16[128,256]{1,0:T(8,128)(2,1)S(1)} %get-tuple-element.49), channel_id=1, source_target_pairs={{0,9},{1,8},{2,11},{3,10},{4,13},{5,12},{6,15},{7,14},{8,1},{9,0},... | collective-permute-start | bytes 196616 | tf_op jit(solution)/shard_map/cond/branch_0_fun/ppermute | solution.py:50
  20.2 1.2 %own_terms.2 = (f32[128,256]{1,0:T(8,128)S(1)}, bf16[128,256]{1,0:T(8,128)(2,1)S(1)}, bf16[256,1024]{1,0:T(8,128)(2,1)S(1)}, bf16[256,1024]{1,0:T(8,128)(2,1)S(1)}) custom-call(f32[4,1024]{1,0:T(4,128)S(1)} %get-tuple-element.35.mine_coef, f32[4,1024]{1,0:T(4,128)S(1)} %get-tuple-element.40.coef_ref, f32[256,1024]{1,0:T(8,128)S(1)} %get-tuple-element.41.e_own, ...), custom_call_target="tpu_custom_call" | custom-call | flops 1048576 | bytes 1024 | tf_op jit(solution)/shard_map/cond/branch_0_fun/own_terms/pallas_call | solution.py:520
  21.4 0.3 collective-permute-start.17
  21.7 2.8 %collective-permute-start.18 = (bf16[128,256]{1,0:T(8,128)(2,1)S(1)}, bf16[128,256]{1,0:T(8,128)(2,1)S(1)}, u32[]{:S(2)}, u32[]{:S(2)}) collective-permute-start(bf16[128,256]{1,0:T(8,128)(2,1)S(1)} %get-tuple-element.52), channel_id=1, source_target_pairs={{0,17},{1,16},{2,19},{3,18},{4,21},{5,20},{6,23},{7,22},{8,25},{9,... | collective-permute-start | bytes 196616 | tf_op jit(solution)/shard_map/cond/branch_0_fun/ppermute | solution.py:50
  24.6 0.9 %collective-permute-start.19 = (bf16[128,256]{1,0:T(8,128)(2,1)S(1)}, bf16[128,256]{1,0:T(8,128)(2,1)S(1)}, u32[]{:S(2)}, u32[]{:S(2)}) collective-permute-start(bf16[128,256]{1,0:T(8,128)(2,1)S(1)} %get-tuple-element.53), channel_id=1, source_target_pairs={{0,16},{4,20},{8,24},{12,28},{16,0},{20,4},{24,8},{28,12},{1,17},{... | collective-permute-start | bytes 196616 | tf_op jit(solution)/shard_map/cond/branch_0_fun/ppermute | solution.py:50
  25.5 0.6 %query_grads.2 = (f32[4,256,128]{2,1,0:T(8,128)S(1)}, bf16[4,256,128]{2,1,0:T(8,128)(2,1)S(1)}) custom-call(bf16[256,256]{1,0:T(8,128)(2,1)S(1)} %get-tuple-element.14.own_ref, bf16[256,256]{1,0:T(8,128)(2,1)S(1)} %broadcast_select_fusion.two_ref, bf16[256,1024]{1,0:T(8,128)(2,1)S(1)} %get-tuple-element.55.ds_own, ...), custom_call_target="tpu_custom_call" | custom-call | flops 1048576 | bytes 1024 | tf_op jit(solution)/shard_map/cond/branch_0_fun/query_grads/pallas_call | solution.py:532
  26.1 0.3 collective-permute-done.17.pair_ref
  26.4 1.1 %collective-permute-done.18.four_ref = bf16[128,256]{1,0:T(8,128)(2,1)S(1)} collective-permute-done((bf16[128,256]{1,0:T(8,128)(2,1)S(1)}, bf16[128,256]{1,0:T(8,128)(2,1)S(1)}, u32[]{:S(2)}, u32[]{:S(2)}) %collective-permute-start.18) | collective-permute-done | bytes 65568 | tf_op jit(solution)/shard_map/cond/branch_0_fun/ppermute | solution.py:50
  27.5 1.4 %collective-permute-done.19.back_ref = bf16[128,256]{1,0:T(8,128)(2,1)S(1)} collective-permute-done((bf16[128,256]{1,0:T(8,128)(2,1)S(1)}, bf16[128,256]{1,0:T(8,128)(2,1)S(1)}, u32[]{:S(2)}, u32[]{:S(2)}) %collective-permute-start.19) | collective-permute-done | bytes 65568 | tf_op jit(solution)/shard_map/cond/branch_0_fun/ppermute | solution.py:50
  29.0 0.1 collective-permute-start.21
  29.0 2.7 %collective-permute-start.20 = (bf16[64,256]{1,0:T(8,128)(2,1)S(1)}, bf16[64,256]{1,0:T(8,128)(2,1)S(1)}, u32[]{:S(2)}, u32[]{:S(2)}) collective-permute-start(bf16[64,256]{1,0:T(8,128)(2,1)S(1)} %get-tuple-element.54), channel_id=1, source_target_pairs={{0,2},{1,3},{2,0},{3,1},{4,6},{5,7},{6,4},{7,5},{8,10},{9,11},{10,... | collective-permute-start | bytes 98312 | tf_op jit(solution)/shard_map/cond/branch_0_fun/ppermute | solution.py:50
  31.7 0.7 %add_grads.2 = bf16[4,256,128]{2,1,0:T(8,128)(2,1)} custom-call(f32[4,256,128]{2,1,0:T(8,128)S(1)} %get-tuple-element.60.mine_ref, bf16[4,256,128]{2,1,0:T(8,128)(2,1)S(1)} %collective-permute-done.21.taken_ref), custom_call_target="tpu_custom_call" | custom-call | flops 1048576 | bytes 1024 | tf_op jit(solution)/shard_map/cond/branch_0_fun/add_grads/pallas_call | solution.py:555
  32.4 1.5 %collective-permute-done.20.taken_ref = bf16[64,256]{1,0:T(8,128)(2,1)S(1)} collective-permute-done((bf16[64,256]{1,0:T(8,128)(2,1)S(1)}, bf16[64,256]{1,0:T(8,128)(2,1)S(1)}, u32[]{:S(2)}, u32[]{:S(2)}) %collective-permute-start.20) | collective-permute-done | bytes 32800 | tf_op jit(solution)/shard_map/cond/branch_0_fun/ppermute | solution.py:50
  33.9 0.6 %last.2 = (bf16[2,64,128]{2,1,0:T(8,128)(2,1)}, bf16[2,64,128]{2,1,0:T(8,128)(2,1)}) custom-call(bf16[64,256]{1,0:T(8,128)(2,1)S(1)} %get-tuple-element.65.here_ref, bf16[64,256]{1,0:T(8,128)(2,1)S(1)} %collective-permute-done.20.taken_ref), custom_call_target="tpu_custom_call" | custom-call | flops 1048576 | bytes 1024 | tf_op jit(solution)/shard_map/cond/branch_0_fun/last/pallas_call | solution.py:560
  (12 shorter events, 0.2 us)
Async XLA Ops:
  2.5 7.8 %collective-permute-start.11 = (bf16[8,256,128]{2,1,0:T(8,128)(2,1)S(1)}, bf16[8,256,128]{2,1,0:T(8,128)(2,1)S(1)}, u32[]{:S(2)}, u32[]{:S(2)}) collective-permute-start(bf16[8,256,128]{2,1,0:T(8,128)(2,1)S(1)} %get-tuple-element.13.rows_ref.refs_7_), channel_id=1, source_target_pairs={{0,4},{4,0},{8,12},{12,8},{16,20},{20,16},{24,28},{28,24},{1,5},{5... | collective-permute-start | bytes 1572872 | tf_op jit(solution)/shard_map/cond/branch_0_fun/ppermute | solution.py:50
  3.1 6.7 %collective-permute-start.12 = (bf16[256,256]{1,0:T(8,128)(2,1)S(1)}, bf16[256,256]{1,0:T(8,128)(2,1)S(1)}, u32[]{:S(2)}, u32[]{:S(2)}) collective-permute-start(bf16[256,256]{1,0:T(8,128)(2,1)S(1)} %get-tuple-element.14.own_ref), channel_id=1, source_target_pairs={{0,16},{4,20},{8,24},{12,28},{16,0},{20,4},{24,8},{28,12},{1,17},{... | collective-permute-start | bytes 393224 | tf_op jit(solution)/shard_map/cond/branch_0_fun/ppermute | solution.py:50
  5.7 6.3 %collective-permute-start.10 = (bf16[256,256]{1,0:T(8,128)(2,1)S(1)}, bf16[256,256]{1,0:T(8,128)(2,1)S(1)}, u32[]{:S(2)}, u32[]{:S(2)}) collective-permute-start(bf16[256,256]{1,0:T(8,128)(2,1)S(1)} %get-tuple-element.14.own_ref), channel_id=1, source_target_pairs={{0,8},{4,12},{8,0},{12,4},{16,24},{20,28},{24,16},{28,20},{1,9},{5... | collective-permute-start | bytes 393224 | tf_op jit(solution)/shard_map/cond/branch_0_fun/ppermute | solution.py:50
  7.1 6.6 %collective-permute-start.9 = (bf16[256,256]{1,0:T(8,128)(2,1)S(1)}, bf16[256,256]{1,0:T(8,128)(2,1)S(1)}, u32[]{:S(2)}, u32[]{:S(2)}) collective-permute-start(bf16[256,256]{1,0:T(8,128)(2,1)S(1)} %get-tuple-element.14.own_ref), channel_id=1, source_target_pairs={{0,24},{4,28},{8,16},{12,20},{16,8},{20,12},{24,0},{28,4},{1,25},{... | collective-permute-start | bytes 393224 | tf_op jit(solution)/shard_map/cond/branch_0_fun/ppermute | solution.py:50
  14.3 1.2 %collective-permute-start.13 = (f32[4,1024]{1,0:T(4,128)S(1)}, f32[4,1024]{1,0:T(4,128)S(1)}, u32[]{:S(2)}, u32[]{:S(2)}) collective-permute-start(f32[4,1024]{1,0:T(4,128)S(1)} %get-tuple-element.29.others_ref), channel_id=1, source_target_pairs={{0,4},{4,0},{8,12},{12,8},{16,20},{20,16},{24,28},{28,24},{1,5},{5... | collective-permute-start | bytes 49160 | tf_op jit(solution)/shard_map/cond/branch_0_fun/ppermute | solution.py:50
  15.0 1.4 %collective-permute-start.14 = (f32[4,1024]{1,0:T(4,128)S(1)}, f32[4,1024]{1,0:T(4,128)S(1)}, u32[]{:S(2)}, u32[]{:S(2)}) collective-permute-start(f32[4,1024]{1,0:T(4,128)S(1)} %get-tuple-element.26.mine_ref), channel_id=1, source_target_pairs={{0,4},{4,0},{8,12},{12,8},{16,20},{20,16},{24,28},{28,24},{1,5},{5... | collective-permute-start | bytes 49160 | tf_op jit(solution)/shard_map/cond/branch_0_fun/ppermute | solution.py:50
  16.9 7.7 %collective-permute-start.15 = (bf16[128,256]{1,0:T(8,128)(2,1)S(1)}, bf16[128,256]{1,0:T(8,128)(2,1)S(1)}, u32[]{:S(2)}, u32[]{:S(2)}) collective-permute-start(bf16[128,256]{1,0:T(8,128)(2,1)S(1)} %get-tuple-element.48), channel_id=1, source_target_pairs={{0,8},{4,12},{8,0},{12,4},{16,24},{20,28},{24,16},{28,20},{1,9},{5... | collective-permute-start | bytes 196616 | tf_op jit(solution)/shard_map/cond/branch_0_fun/ppermute | solution.py:50
  18.7 5.9 %collective-permute-start.16 = (bf16[128,256]{1,0:T(8,128)(2,1)S(1)}, bf16[128,256]{1,0:T(8,128)(2,1)S(1)}, u32[]{:S(2)}, u32[]{:S(2)}) collective-permute-start(bf16[128,256]{1,0:T(8,128)(2,1)S(1)} %get-tuple-element.49), channel_id=1, source_target_pairs={{0,9},{1,8},{2,11},{3,10},{4,13},{5,12},{6,15},{7,14},{8,1},{9,0},... | collective-permute-start | bytes 196616 | tf_op jit(solution)/shard_map/cond/branch_0_fun/ppermute | solution.py:50
  21.4 5.0 %collective-permute-start.17 = (bf16[128,256]{1,0:T(8,128)(2,1)S(1)}, bf16[128,256]{1,0:T(8,128)(2,1)S(1)}, u32[]{:S(2)}, u32[]{:S(2)}) collective-permute-start(bf16[128,256]{1,0:T(8,128)(2,1)S(1)} %get-tuple-element.51), channel_id=1, source_target_pairs={{0,1},{1,0},{2,3},{3,2},{4,5},{5,4},{6,7},{7,6},{8,9},{9,8},{10,11... | collective-permute-start | bytes 196616 | tf_op jit(solution)/shard_map/cond/branch_0_fun/ppermute | solution.py:50
  21.7 5.8 %collective-permute-start.18 = (bf16[128,256]{1,0:T(8,128)(2,1)S(1)}, bf16[128,256]{1,0:T(8,128)(2,1)S(1)}, u32[]{:S(2)}, u32[]{:S(2)}) collective-permute-start(bf16[128,256]{1,0:T(8,128)(2,1)S(1)} %get-tuple-element.52), channel_id=1, source_target_pairs={{0,17},{1,16},{2,19},{3,18},{4,21},{5,20},{6,23},{7,22},{8,25},{9,... | collective-permute-start | bytes 196616 | tf_op jit(solution)/shard_map/cond/branch_0_fun/ppermute | solution.py:50
  24.6 4.3 %collective-permute-start.19 = (bf16[128,256]{1,0:T(8,128)(2,1)S(1)}, bf16[128,256]{1,0:T(8,128)(2,1)S(1)}, u32[]{:S(2)}, u32[]{:S(2)}) collective-permute-start(bf16[128,256]{1,0:T(8,128)(2,1)S(1)} %get-tuple-element.53), channel_id=1, source_target_pairs={{0,16},{4,20},{8,24},{12,28},{16,0},{20,4},{24,8},{28,12},{1,17},{... | collective-permute-start | bytes 196616 | tf_op jit(solution)/shard_map/cond/branch_0_fun/ppermute | solution.py:50
  29.0 2.7 %collective-permute-start.21 = (bf16[4,256,128]{2,1,0:T(8,128)(2,1)S(1)}, bf16[4,256,128]{2,1,0:T(8,128)(2,1)S(1)}, u32[]{:S(2)}, u32[]{:S(2)}) collective-permute-start(bf16[4,256,128]{2,1,0:T(8,128)(2,1)S(1)} %get-tuple-element.63), channel_id=1, source_target_pairs={{0,4},{4,0},{8,12},{12,8},{16,20},{20,16},{24,28},{28,24},{1,5},{5... | collective-permute-start | bytes 786440 | tf_op jit(solution)/shard_map/cond/branch_0_fun/ppermute | solution.py:50
  29.0 4.9 %collective-permute-start.20 = (bf16[64,256]{1,0:T(8,128)(2,1)S(1)}, bf16[64,256]{1,0:T(8,128)(2,1)S(1)}, u32[]{:S(2)}, u32[]{:S(2)}) collective-permute-start(bf16[64,256]{1,0:T(8,128)(2,1)S(1)} %get-tuple-element.54), channel_id=1, source_target_pairs={{0,2},{1,3},{2,0},{3,1},{4,6},{5,7},{6,4},{7,5},{8,10},{9,11},{10,... | collective-permute-start | bytes 98312 | tf_op jit(solution)/shard_map/cond/branch_0_fun/ppermute | solution.py:50
where the time goes:
time: 34.7 us; the launch traced here: 34.6 us
  starting transfers between devices  15.3 us (44%)
  waiting for transfers between devices  9.01 us (26%)
  Pallas kernels  8.81 us (25%)
  between operations  1.29 us (4%)
    ppermute x13, starting transfers between devices, exchanged(): return lax.ppermute(block, axis, [(i, i ^ mask) for i in range(count)])  15.3 us
    ppermute x13, waiting for transfers between devices, exchanged(): return lax.ppermute(block, axis, [(i, i ^ mask) for i in range(count)])  9.01 us
    pallas_call x1, Pallas kernels, per_device(): pl.pallas_call(functools.partial(prepare_body, GROUP // heads, middle), o...  1.24 us
    pallas_call x1, Pallas kernels, gradients(): call(far_own_terms_body, 'own_terms', [VMEM] * 8, (part, halves[1], half,...  1.18 us
    pallas_call x1, Pallas kernels, gradients(): call(functools.partial(my_terms_body, len(mine_stats)), 'my_terms', [VMEM...  0.78 us
    pallas_call x1, Pallas kernels, gradients(): call(add_grads_body, 'add_grads', [VMEM] * 2, (shape(all_rows, bf16),))  0.75 us
  transfers between devices with their start and end apart: 13, of which 7 were waited for; matrix products, arithmetic and copies ran while one was open for 0% of the time, Pallas kernels for 17%

commit v1 on v0

--- a/solution.py
+++ b/solution.py
@@ -330,7 +330,7 @@
     out_ref[...] = sum_ref[...] + pair_ref[...].astype(f32) + taken
 
 
-def relay_body(kept_ref, four_ref, two_ref, two_pair_ref, out_ref, sent_ref):
+def relay_body(kept_ref, four_ref, two_pair_ref, two_ref, out_ref, sent_ref):
     ctx = lax.axis_index("ctx")
     taken = two_ref[...].astype(f32) + two_pair_ref[...].astype(f32)
     out_ref[...] = kept_ref[...] + jnp.where(ctx & 2 == 0, taken, 0.0)
@@ -537,7 +537,7 @@
     if far:
         own_kept, relayed = call(
             relay_body, "relay", [VMEM] * 4, (part, halves[0]),
-        )(own_kept, four_kept, two_back, two_pair)
+        )(own_kept, four_kept, two_pair, two_back)
         four_back = exchanged(relayed, "ctx", 4)
         own_kept, = call(functools.partial(add_others_body, owns_four), "add_others", [VMEM] * 3,
                          (part,))(own_kept, own_pair, four_pair)

time: 34.7 us -> 27.6 us (0.80)
  starting transfers between devices: 15.3 us -> 10.1 us
  Pallas kernels: 8.81 us -> 7.66 us
  waiting for transfers between devices: 9.01 us -> 8.32 us
    ppermute x13 -> x9, starting transfers between devices: 15.3 us -> 10.1 us  [exchanged(): return lax.ppermute(block, axis, [(i, i ^ mask) for i in range(count)])]
    pallas_call x6 -> x3, Pallas kernels: 2.47 us -> 1.29 us  [the longest x1 0.63 us: gradients(): call(near_own_terms_body, 'own_terms', [VMEM] * 5, (part, halves[1], half...]
    ppermute x13 -> x9, waiting for transfers between devices: 9.01 us -> 8.32 us  [exchanged(): return lax.ppermute(block, axis, [(i, i ^ mask) for i in range(count)])]
  transfers between devices with their start and end apart: 13 -> 9, of which waited for: 7 -> 5; matrix products, arithmetic and copies ran while one was open for 0% -> 0% of each run, Pallas kernels for 17% -> 17%
where the time goes in v1:
time: 27.6 us; the launch traced here: 27.4 us
  starting transfers between devices  10.1 us (37%)
  waiting for transfers between devices  8.32 us (30%)
  Pallas kernels  7.66 us (28%)
  between operations  1.29 us (5%)
    ppermute x9, starting transfers between devices, exchanged(): return lax.ppermute(block, axis, [(i, i ^ mask) for i in range(count)])  10.1 us
    ppermute x9, waiting for transfers between devices, exchanged(): return lax.ppermute(block, axis, [(i, i ^ mask) for i in range(count)])  8.32 us
    pallas_call x1, Pallas kernels, per_device(): pl.pallas_call(functools.partial(prepare_body, GROUP // heads, middle), o...  1.24 us
    pallas_call x1, Pallas kernels, gradients(): call(functools.partial(my_terms_body, len(mine_stats)), 'my_terms', [VMEM...  0.89 us
    pallas_call x1, Pallas kernels, gradients(): call(add_grads_body, 'add_grads', [VMEM] * 2, (shape(all_rows, bf16),))  0.75 us
    pallas_call x1, Pallas kernels, gradients(): call(functools.partial(last_body, share), 'last', [VMEM] * 2, (shape((gro...  0.64 us
    pallas_call x1, Pallas kernels, gradients(): call(near_own_terms_body, 'own_terms', [VMEM] * 5, (part, halves[1], half...  0.63 us
    pallas_call x1, Pallas kernels, gradients(): call(own_unit_body, 'own_unit', [VMEM] * 3, (flipped, wide, wide, stats))  0.63 us
  transfers between devices with their start and end apart: 9, of which 5 were waited for; matrix products, arithmetic and copies ran while one was open for 0% of the time, Pallas kernels for 17%

profile of v1, /device:TPU:0, one launch (start us, length us, event | category | flops | bytes accessed | tf_op | source)
XLA Modules:
  0.0 27.4 jit_solution(14641884415009288391)
XLA Ops:
  0.6 1.2 %prepare.1 = (s32[1]{0:T(128)}, s32[2,256]{1,0:T(2,128)S(1)}, bf16[256,256]{1,0:T(8,128)(2,1)S(1)}, bf16[8,256,128]{2,1,0:T(8,128)(2,1)S(1)}) custom-call(s32[4]{0:T(128)} %lengths_in.1, bf16[2,256,128]{2,1,0:T(8,128)(2,1)} %keys_ref.1, bf16[2,256,128]{2,1,0:T(8,128)(2,1)} %values_ref.1, bf16[4,256,128]{2,1,0:T(8,128)(2,1)} %queries_ref.1, ...), custom_call_target="tpu_custom_call" | custom-call | tf_op jit(solution)/shard_map/prepare/pallas_call | solution.py:402
  2.5 24.9 %conditional.1 = (bf16[4,256,128]{2,1,0:T(8,128)(2,1)}, bf16[2,64,128]{2,1,0:T(8,128)(2,1)}, bf16[2,64,128]{2,1,0:T(8,128)(2,1)}) conditional(s32[]{:T(128)} %bitcast, (s32[2,256]{1,0:T(2,128)S(1)}, bf16[8,256,128]{2,1,0:T(8,128)(2,1)S(1)}, bf16[256,256]{1,0:T(8,128)(2,1)S(1)}) %tuple.23, (bf16[8,256,128]{2,1,0:T(8,128)(2,1)S(1)}, ...), branch_computations={%region_0.1_spmd, %region_1.2_spmd} | conditional | flops 15794181 | bytes 6700630 | solution.py:416
  2.5 0.5 %collective-permute-start = (bf16[8,256,128]{2,1,0:T(8,128)(2,1)S(1)}, bf16[8,256,128]{2,1,0:T(8,128)(2,1)S(1)}, u32[]{:S(2)}, u32[]{:S(2)}) collective-permute-start(bf16[8,256,128]{2,1,0:T(8,128)(2,1)S(1)} %get-tuple-element.70.rows_ref.refs_6_), channel_id=1, source_target_pairs={{0,4},{4,0},{8,12},{12,8},{16,20},{20,16},{24,28},{28,24},{1,5},{5... | collective-permute-start | bytes 1572872 | tf_op jit(solution)/shard_map/cond/branch_1_fun/ppermute | solution.py:50
  3.1 2.6 %collective-permute-start.1 = (bf16[256,256]{1,0:T(8,128)(2,1)S(1)}, bf16[256,256]{1,0:T(8,128)(2,1)S(1)}, u32[]{:S(2)}, u32[]{:S(2)}) collective-permute-start(bf16[256,256]{1,0:T(8,128)(2,1)S(1)} %get-tuple-element.71.own_ref), channel_id=1, source_target_pairs={{0,8},{4,12},{8,0},{12,4},{16,24},{20,28},{24,16},{28,20},{1,9},{5... | collective-permute-start | bytes 393224 | tf_op jit(solution)/shard_map/cond/branch_1_fun/ppermute | solution.py:50
  5.6 0.6 %own_unit.3 = (bf16[8,128,256]{2,1,0:T(8,128)(2,1)S(1)}, f32[256,1024]{1,0:T(8,128)S(1)}, f32[256,1024]{1,0:T(8,128)S(1)}, f32[3,1024]{1,0:T(4,128)S(1)}) custom-call(s32[2,256]{1,0:T(2,128)S(1)} %get-tuple-element.69.starts_ref, bf16[8,256,128]{2,1,0:T(8,128)(2,1)S(1)} %get-tuple-element.70.rows_ref.refs_6_, bf16[256,256]{1,0:T(8,128)(2,1)S(1)} %get-tuple-element.71.own_ref), custom_call_target="tpu_custom_call" | custom-call | flops 1048576 | bytes 1024 | tf_op jit(solution)/shard_map/cond/branch_1_fun/own_unit/pallas_call | solution.py:442
  6.3 0.0 collective-permute-done.other_rows
  6.3 0.6 %side_unit.3 = (bf16[8,128,256]{2,1,0:T(8,128)(2,1)S(1)}, f32[256,1024]{1,0:T(8,128)S(1)}, f32[256,1024]{1,0:T(8,128)S(1)}, f32[3,1024]{1,0:T(4,128)S(1)}) custom-call(s32[2,256]{1,0:T(2,128)S(1)} %get-tuple-element.69.starts_ref, bf16[8,256,128]{2,1,0:T(8,128)(2,1)S(1)} %collective-permute-done.other_rows, bf16[256,256]{1,0:T(8,128)(2,1)S(1)} %get-tuple-element.71.own_ref), custom_call_target="tpu_custom_call" | custom-call | flops 1048576 | bytes 1024 | tf_op jit(solution)/shard_map/cond/branch_1_fun/side_unit/pallas_call | solution.py:455
  6.9 2.8 %collective-permute-done.1.two_ref = bf16[256,256]{1,0:T(8,128)(2,1)S(1)} collective-permute-done((bf16[256,256]{1,0:T(8,128)(2,1)S(1)}, bf16[256,256]{1,0:T(8,128)(2,1)S(1)}, u32[]{:S(2)}, u32[]{:S(2)}) %collective-permute-start.1) | collective-permute-done | bytes 131104 | tf_op jit(solution)/shard_map/cond/branch_1_fun/ppermute | solution.py:50
  9.7 0.6 %cross_unit.3 = (f32[256,1024]{1,0:T(8,128)S(1)}, f32[256,1024]{1,0:T(8,128)S(1)}, f32[3,1024]{1,0:T(4,128)S(1)}, f32[4,1024]{1,0:T(4,128)S(1)}) custom-call(s32[2,256]{1,0:T(2,128)S(1)} %get-tuple-element.69.starts_ref, bf16[8,128,256]{2,1,0:T(8,128)(2,1)S(1)} %get-tuple-element.72.turned_ref, bf16[256,256]{1,0:T(8,128)(2,1)S(1)} %collective-permute-done.1.two_ref, ...), custom_call_target="tpu_custom_call" | custom-call | flops 1048576 | bytes 1024 | tf_op jit(solution)/shard_map/cond/branch_1_fun/cross_unit/pallas_call | solution.py:462
  10.3 0.1 collective-permute-start.3
  10.4 0.6 %two_unit.3 = (f32[256,1024]{1,0:T(8,128)S(1)}, f32[256,1024]{1,0:T(8,128)S(1)}, f32[3,1024]{1,0:T(4,128)S(1)}, f32[4,1024]{1,0:T(4,128)S(1)}) custom-call(s32[2,256]{1,0:T(2,128)S(1)} %get-tuple-element.69.starts_ref, bf16[8,128,256]{2,1,0:T(8,128)(2,1)S(1)} %get-tuple-element.78.turned_ref, bf16[256,256]{1,0:T(8,128)(2,1)S(1)} %collective-permute-done.1.two_ref, ...), custom_call_target="tpu_custom_call" | custom-call | flops 1048576 | bytes 1024 | tf_op jit(solution)/shard_map/cond/branch_1_fun/two_unit/pallas_call | solution.py:466
  11.0 0.6 %collective-permute-start.2 = (f32[4,1024]{1,0:T(4,128)S(1)}, f32[4,1024]{1,0:T(4,128)S(1)}, u32[]{:S(2)}, u32[]{:S(2)}) collective-permute-start(f32[4,1024]{1,0:T(4,128)S(1)} %get-tuple-element.80.mine_ref), channel_id=1, source_target_pairs={{0,4},{4,0},{8,12},{12,8},{16,20},{20,16},{24,28},{28,24},{1,5},{5... | collective-permute-start | bytes 49160 | tf_op jit(solution)/shard_map/cond/branch_1_fun/ppermute | solution.py:50
  11.5 0.0 collective-permute-done.3.taken_ref
  11.5 0.9 %my_terms.3 = (f32[4,1024]{1,0:T(4,128)}, bf16[256,1024]{1,0:T(8,128)(2,1)S(1)}, bf16[256,1024]{1,0:T(8,128)(2,1)S(1)}, f32[256,256]{1,0:T(8,128)S(1)}, f32[256,256]{1,0:T(8,128)S(1)}) custom-call(f32[4,1024]{1,0:T(4,128)S(1)} %get-tuple-element.80.mine_ref, f32[4,1024]{1,0:T(4,128)S(1)} %collective-permute-done.3.taken_ref, ...), custom_call_target="tpu_custom_call" | custom-call | flops 1048576 | bytes 1024 | tf_op jit(solution)/shard_map/cond/branch_1_fun/my_terms/pallas_call | solution.py:472
  12.4 0.0 collective-permute-done.2.taken_ref
  12.4 0.5 %two_terms.3 = (f32[4,1024]{1,0:T(4,128)S(1)}, bf16[128,256]{1,0:T(8,128)(2,1)S(1)}, bf16[128,256]{1,0:T(8,128)(2,1)S(1)}, bf16[256,1024]{1,0:T(8,128)(2,1)S(1)}) custom-call(f32[4,1024]{1,0:T(4,128)S(1)} %get-tuple-element.77.others_ref, f32[4,1024]{1,0:T(4,128)S(1)} %collective-permute-done.2.taken_ref, f32[3,1024]{1,0:T(4,128)S(1)} %get-tuple-element.76.stats_side, ...), custom_call_target="tpu_custom_call" | custom-call | flops 1048576 | bytes 1024 | tf_op jit(solution)/shard_map/cond/branch_1_fun/two_terms/pallas_call | solution.py:508
  12.9 1.8 %collective-permute-start.4 = (bf16[128,256]{1,0:T(8,128)(2,1)S(1)}, bf16[128,256]{1,0:T(8,128)(2,1)S(1)}, u32[]{:S(2)}, u32[]{:S(2)}) collective-permute-start(bf16[128,256]{1,0:T(8,128)(2,1)S(1)} %get-tuple-element.95), channel_id=1, source_target_pairs={{0,8},{4,12},{8,0},{12,4},{16,24},{20,28},{24,16},{28,20},{1,9},{5... | collective-permute-start | bytes 196616 | tf_op jit(solution)/shard_map/cond/branch_1_fun/ppermute | solution.py:50
  14.8 1.6 %collective-permute-start.5 = (bf16[128,256]{1,0:T(8,128)(2,1)S(1)}, bf16[128,256]{1,0:T(8,128)(2,1)S(1)}, u32[]{:S(2)}, u32[]{:S(2)}) collective-permute-start(bf16[128,256]{1,0:T(8,128)(2,1)S(1)} %get-tuple-element.96), channel_id=1, source_target_pairs={{0,9},{1,8},{2,11},{3,10},{4,13},{5,12},{6,15},{7,14},{8,1},{9,0},... | collective-permute-start | bytes 196616 | tf_op jit(solution)/shard_map/cond/branch_1_fun/ppermute | solution.py:50
  16.3 0.6 %own_terms.3 = (f32[128,256]{1,0:T(8,128)S(1)}, bf16[128,256]{1,0:T(8,128)(2,1)S(1)}, bf16[256,1024]{1,0:T(8,128)(2,1)S(1)}) custom-call(f32[4,1024]{1,0:T(4,128)S(1)} %get-tuple-element.90.coef_ref, f32[256,1024]{1,0:T(8,128)S(1)} %get-tuple-element.91.e_side, f32[256,1024]{1,0:T(8,128)S(1)} %get-tuple-element.92.dp_side, ...), custom_call_target="tpu_custom_call" | custom-call | flops 1048576 | bytes 1024 | tf_op jit(solution)/shard_map/cond/branch_1_fun/own_terms/pallas_call | solution.py:526
  16.9 0.2 collective-permute-start.6
  17.2 0.6 %query_grads.3 = (f32[4,256,128]{2,1,0:T(8,128)S(1)}, bf16[4,256,128]{2,1,0:T(8,128)(2,1)S(1)}) custom-call(bf16[256,256]{1,0:T(8,128)(2,1)S(1)} %get-tuple-element.71.own_ref, bf16[256,256]{1,0:T(8,128)(2,1)S(1)} %collective-permute-done.1.two_ref, bf16[256,1024]{1,0:T(8,128)(2,1)S(1)} %get-tuple-element.99.ds_own, ...), custom_call_target="tpu_custom_call" | custom-call | flops 1048576 | bytes 1024 | tf_op jit(solution)/shard_map/cond/branch_1_fun/query_grads/pallas_call | solution.py:532
  17.8 0.2 collective-permute-done.4.two_ref
  18.0 2.1 %collective-permute-done.5.two_pair_ref = bf16[128,256]{1,0:T(8,128)(2,1)S(1)} collective-permute-done((bf16[128,256]{1,0:T(8,128)(2,1)S(1)}, bf16[128,256]{1,0:T(8,128)(2,1)S(1)}, u32[]{:S(2)}, u32[]{:S(2)}) %collective-permute-start.5) | collective-permute-done | bytes 65568 | tf_op jit(solution)/shard_map/cond/branch_1_fun/ppermute | solution.py:50
  20.1 1.2 %collective-permute-done.6.back_ref = bf16[128,256]{1,0:T(8,128)(2,1)S(1)} collective-permute-done((bf16[128,256]{1,0:T(8,128)(2,1)S(1)}, bf16[128,256]{1,0:T(8,128)(2,1)S(1)}, u32[]{:S(2)}, u32[]{:S(2)}) %collective-permute-start.6) | collective-permute-done | bytes 65568 | tf_op jit(solution)/shard_map/cond/branch_1_fun/ppermute | solution.py:50
  21.3 0.1 collective-permute-start.8
  21.4 2.7 %collective-permute-start.7 = (bf16[64,256]{1,0:T(8,128)(2,1)S(1)}, bf16[64,256]{1,0:T(8,128)(2,1)S(1)}, u32[]{:S(2)}, u32[]{:S(2)}) collective-permute-start(bf16[64,256]{1,0:T(8,128)(2,1)S(1)} %get-tuple-element.98), channel_id=1, source_target_pairs={{0,2},{1,3},{2,0},{3,1},{4,6},{5,7},{6,4},{7,5},{8,10},{9,11},{10,... | collective-permute-start | bytes 98312 | tf_op jit(solution)/shard_map/cond/branch_1_fun/ppermute | solution.py:50
  24.0 0.0 collective-permute-done.8.taken_ref
  24.0 0.7 %add_grads.3 = bf16[4,256,128]{2,1,0:T(8,128)(2,1)} custom-call(f32[4,256,128]{2,1,0:T(8,128)S(1)} %get-tuple-element.103.mine_ref, bf16[4,256,128]{2,1,0:T(8,128)(2,1)S(1)} %collective-permute-done.8.taken_ref), custom_call_target="tpu_custom_call" | custom-call | flops 1048576 | bytes 1024 | tf_op jit(solution)/shard_map/cond/branch_1_fun/add_grads/pallas_call | solution.py:555
  24.8 2.0 %collective-permute-done.7.taken_ref = bf16[64,256]{1,0:T(8,128)(2,1)S(1)} collective-permute-done((bf16[64,256]{1,0:T(8,128)(2,1)S(1)}, bf16[64,256]{1,0:T(8,128)(2,1)S(1)}, u32[]{:S(2)}, u32[]{:S(2)}) %collective-permute-start.7) | collective-permute-done | bytes 32800 | tf_op jit(solution)/shard_map/cond/branch_1_fun/ppermute | solution.py:50
  26.8 0.6 %last.3 = (bf16[2,64,128]{2,1,0:T(8,128)(2,1)}, bf16[2,64,128]{2,1,0:T(8,128)(2,1)}) custom-call(bf16[64,256]{1,0:T(8,128)(2,1)S(1)} %get-tuple-element.108.here_ref, bf16[64,256]{1,0:T(8,128)(2,1)S(1)} %collective-permute-done.7.taken_ref), custom_call_target="tpu_custom_call" | custom-call | flops 1048576 | bytes 1024 | tf_op jit(solution)/shard_map/cond/branch_1_fun/last/pallas_call | solution.py:560
  (2 shorter events, 0.0 us)
Async XLA Ops:
  2.5 3.7 %collective-permute-start = (bf16[8,256,128]{2,1,0:T(8,128)(2,1)S(1)}, bf16[8,256,128]{2,1,0:T(8,128)(2,1)S(1)}, u32[]{:S(2)}, u32[]{:S(2)}) collective-permute-start(bf16[8,256,128]{2,1,0:T(8,128)(2,1)S(1)} %get-tuple-element.70.rows_ref.refs_6_), channel_id=1, source_target_pairs={{0,4},{4,0},{8,12},{12,8},{16,20},{20,16},{24,28},{28,24},{1,5},{5... | collective-permute-start | bytes 1572872 | tf_op jit(solution)/shard_map/cond/branch_1_fun/ppermute | solution.py:50
  3.1 6.7 %collective-permute-start.1 = (bf16[256,256]{1,0:T(8,128)(2,1)S(1)}, bf16[256,256]{1,0:T(8,128)(2,1)S(1)}, u32[]{:S(2)}, u32[]{:S(2)}) collective-permute-start(bf16[256,256]{1,0:T(8,128)(2,1)S(1)} %get-tuple-element.71.own_ref), channel_id=1, source_target_pairs={{0,8},{4,12},{8,0},{12,4},{16,24},{20,28},{24,16},{28,20},{1,9},{5... | collective-permute-start | bytes 393224 | tf_op jit(solution)/shard_map/cond/branch_1_fun/ppermute | solution.py:50
  10.3 1.2 %collective-permute-start.3 = (f32[4,1024]{1,0:T(4,128)S(1)}, f32[4,1024]{1,0:T(4,128)S(1)}, u32[]{:S(2)}, u32[]{:S(2)}) collective-permute-start(f32[4,1024]{1,0:T(4,128)S(1)} %get-tuple-element.77.others_ref), channel_id=1, source_target_pairs={{0,4},{4,0},{8,12},{12,8},{16,20},{20,16},{24,28},{28,24},{1,5},{5... | collective-permute-start | bytes 49160 | tf_op jit(solution)/shard_map/cond/branch_1_fun/ppermute | solution.py:50
  11.0 1.5 %collective-permute-start.2 = (f32[4,1024]{1,0:T(4,128)S(1)}, f32[4,1024]{1,0:T(4,128)S(1)}, u32[]{:S(2)}, u32[]{:S(2)}) collective-permute-start(f32[4,1024]{1,0:T(4,128)S(1)} %get-tuple-element.80.mine_ref), channel_id=1, source_target_pairs={{0,4},{4,0},{8,12},{12,8},{16,20},{20,16},{24,28},{28,24},{1,5},{5... | collective-permute-start | bytes 49160 | tf_op jit(solution)/shard_map/cond/branch_1_fun/ppermute | solution.py:50
  12.9 5.0 %collective-permute-start.4 = (bf16[128,256]{1,0:T(8,128)(2,1)S(1)}, bf16[128,256]{1,0:T(8,128)(2,1)S(1)}, u32[]{:S(2)}, u32[]{:S(2)}) collective-permute-start(bf16[128,256]{1,0:T(8,128)(2,1)S(1)} %get-tuple-element.95), channel_id=1, source_target_pairs={{0,8},{4,12},{8,0},{12,4},{16,24},{20,28},{24,16},{28,20},{1,9},{5... | collective-permute-start | bytes 196616 | tf_op jit(solution)/shard_map/cond/branch_1_fun/ppermute | solution.py:50
  14.8 5.3 %collective-permute-start.5 = (bf16[128,256]{1,0:T(8,128)(2,1)S(1)}, bf16[128,256]{1,0:T(8,128)(2,1)S(1)}, u32[]{:S(2)}, u32[]{:S(2)}) collective-permute-start(bf16[128,256]{1,0:T(8,128)(2,1)S(1)} %get-tuple-element.96), channel_id=1, source_target_pairs={{0,9},{1,8},{2,11},{3,10},{4,13},{5,12},{6,15},{7,14},{8,1},{9,0},... | collective-permute-start | bytes 196616 | tf_op jit(solution)/shard_map/cond/branch_1_fun/ppermute | solution.py:50
  16.9 4.3 %collective-permute-start.6 = (bf16[128,256]{1,0:T(8,128)(2,1)S(1)}, bf16[128,256]{1,0:T(8,128)(2,1)S(1)}, u32[]{:S(2)}, u32[]{:S(2)}) collective-permute-start(bf16[128,256]{1,0:T(8,128)(2,1)S(1)} %get-tuple-element.97), channel_id=1, source_target_pairs={{0,1},{1,0},{2,3},{3,2},{4,5},{5,4},{6,7},{7,6},{8,9},{9,8},{10,11... | collective-permute-start | bytes 196616 | tf_op jit(solution)/shard_map/cond/branch_1_fun/ppermute | solution.py:50
  21.3 2.7 %collective-permute-start.8 = (bf16[4,256,128]{2,1,0:T(8,128)(2,1)S(1)}, bf16[4,256,128]{2,1,0:T(8,128)(2,1)S(1)}, u32[]{:S(2)}, u32[]{:S(2)}) collective-permute-start(bf16[4,256,128]{2,1,0:T(8,128)(2,1)S(1)} %get-tuple-element.106), channel_id=1, source_target_pairs={{0,4},{4,0},{8,12},{12,8},{16,20},{20,16},{24,28},{28,24},{1,5},{5... | collective-permute-start | bytes 786440 | tf_op jit(solution)/shard_map/cond/branch_1_fun/ppermute | solution.py:50
  21.4 5.4 %collective-permute-start.7 = (bf16[64,256]{1,0:T(8,128)(2,1)S(1)}, bf16[64,256]{1,0:T(8,128)(2,1)S(1)}, u32[]{:S(2)}, u32[]{:S(2)}) collective-permute-start(bf16[64,256]{1,0:T(8,128)(2,1)S(1)} %get-tuple-element.98), channel_id=1, source_target_pairs={{0,2},{1,3},{2,0},{3,1},{4,6},{5,7},{6,4},{7,5},{8,10},{9,11},{10,... | collective-permute-start | bytes 98312 | tf_op jit(solution)/shard_map/cond/branch_1_fun/ppermute | solution.py:50
